TPU v7x, 32 devices: a whole 2x2x4 slice. The times are simulated.
32 devices in a mesh: segment: 4 (over y, x), seq: 4 (over z), mp: 2 (over core).
Axes of the slice: x: 2, y: 2, z: 4, core: 2. Of those that a mesh axis runs over, the one named last changes fastest.
Arguments:
- video: bfloat16 [3, 256, 6144], P(None, 'seq', 'mp'), may hold values from -6 to 6
- caption_kv: bfloat16 [4, 768, 2, 3072], P('segment', 'seq', None, 'mp'), may hold values from -6 to 6
- caption_lengths: int32 [3], replicated, may hold values from 1 to 400, 768 in all
- order: int32 [3], replicated, may hold values from 0 to 2, each once
- gains: float32 [4, 6144], P('segment'), may hold values from 0.25 to 1.75
- w_query: bfloat16 [4, 6144, 3072], P('segment', 'seq', 'mp')
- w_out: bfloat16 [4, 3072, 6144], P('segment', None, 'mp'), may hold values from -0.109375 to 0.109375
Outputs:
- section_out: bfloat16 [4, 3, 256, 6144], P('segment', None, 'seq', 'mp')
Inputs may be any that keep to these rules, and one draw needn't show every extreme that they name: `caption_lengths`: caption lengths sum to 768; the largest is exactly 400. `order`: each sample is named by exactly one micro-batch.
All inputs are finite; a program needn't handle non-finite values.
Results may differ from a plain program's by a relative error of at most 0.009.
Values may be sent and summed in bfloat16 or wider, within the bound.
A program may use at most 128 MiB of HBM per device.

v0:
```python
import jax
import jax.numpy as jnp
from jax import lax
from jax.sharding import PartitionSpec as P

HEAD_DIM = 128


def passed_along(block, axis, distance):
    devices = range(lax.axis_size(axis))
    route = [(i - distance, i) for i in devices if i - distance in devices]
    return lax.ppermute(block, axis, route)


def block_terms(query, kv, start_row, length):
    tokens = query.shape[0]
    heads = query.shape[1] // HEAD_DIM
    count = kv.shape[0]
    qheads = query.reshape(tokens, heads, HEAD_DIM)
    keys = kv[:, 0, :].reshape(count, heads, HEAD_DIM)
    values = kv[:, 1, :].astype(jnp.float32).reshape(count, heads, HEAD_DIM)
    scores = jnp.einsum(
        "thd,rhd->htr", qheads, keys, preferred_element_type=jnp.float32
    ) * HEAD_DIM ** (-0.5)
    rows = jnp.arange(count, dtype=jnp.int32)
    valid = (rows >= start_row) & (rows < start_row + length)
    scores = jnp.where(valid[None, None, :], scores, -1e30)
    top = jnp.max(scores, axis=-1)
    weights = jnp.where(valid[None, None, :], jnp.exp(scores - top[:, :, None]), 0.0)
    total = jnp.sum(weights, axis=-1)
    acc = jnp.einsum("htr,rhd->htd", weights, values)
    return (top, total, acc)


def finish(total, acc):
    heads, tokens, width = acc.shape
    result = acc / total[:, :, None]
    return jnp.transpose(result, (1, 0, 2)).reshape(tokens, heads * width).astype(jnp.bfloat16)


def body(video, caption_kv, caption_lengths, order, gains, w_query, w_out):
    samples = video.shape[0]
    segments = lax.axis_size("segment")
    here = lax.axis_index("segment")
    gain = gains[0]
    w_local = w_query[0]
    out_weight = w_out[0]
    kv_local = caption_kv[0]
    offsets = jnp.cumsum(caption_lengths) - caption_lengths
    w_whole = lax.all_gather(w_local, "seq", axis=0, tiled=True)
    kv_whole = lax.all_gather(kv_local, "seq", axis=0, tiled=True)
    received = jnp.zeros_like(video[0])
    section_out = jnp.zeros_like(video)
    for tick in range(samples + segments - 1):
        micro = tick - here
        active = (micro >= 0) & (micro < samples)
        slot = jnp.clip(micro, 0, samples - 1)
        sample = order[slot]
        first = lax.dynamic_index_in_dim(video, sample, 0, keepdims=False)
        current = jnp.where(here == 0, first, received)
        whole = lax.all_gather(current, "mp", axis=1, tiled=True)
        wholef = whole.astype(jnp.float32)
        meansq = jnp.mean(wholef * wholef, axis=-1, keepdims=True)
        normed = (wholef * lax.rsqrt(meansq + 1e-06) * gain).astype(jnp.bfloat16)
        query = jnp.dot(normed, w_whole, preferred_element_type=jnp.float32)
        query = query.astype(jnp.bfloat16)
        start_row = offsets[sample]
        length = caption_lengths[sample]
        top, total, acc = block_terms(query, kv_whole, start_row, length)
        attended = finish(total, acc)
        projected = jnp.dot(
            lax.all_gather(attended, "mp", axis=1, tiled=True),
            out_weight,
            preferred_element_type=jnp.float32,
        )
        mixed = (current.astype(jnp.float32) + projected).astype(jnp.bfloat16)
        updated = lax.dynamic_update_index_in_dim(section_out, mixed, slot, 0)
        section_out = jnp.where(active, updated, section_out)
        received = passed_along(mixed, "segment", 1)
    return section_out[None]


def solution(mesh):
    in_specs = (
        P(None, "seq", "mp"),
        P("segment", "seq", None, "mp"),
        P(),
        P(),
        P("segment", None),
        P("segment", "seq", "mp"),
        P("segment", None, "mp"),
    )
    out_specs = P("segment", None, "seq", "mp")
    return jax.shard_map(body, mesh=mesh, in_specs=in_specs, out_specs=out_specs, check_vma=False)
```

profile of v0, /device:TPU:7, one launch (start us, length us, event | category | flops | bytes accessed | tf_op | source)
XLA Modules:
  0.0 639.0 jit_solution(13306959958078002717)
XLA Ops:
  24.5 2.7 all-gather
  27.4 72.3 %all-gather.8.cloned.1.call-done = bf16[1,768,2,1536]{3,2,0,1:T(2,128)(2,1)} async-done(((bf16[1,192,2,1536]{3,2,0,1:T(2,128)(2,1)}), bf16[1,768,2,1536]{3,2,0,1:T(2,128)(2,1)}) %all-gather.8.cloned.1.call-update) | async-done | bytes 4718608 | tf_op jit(solution)/shard_map/all_gather | solution.py:51
  99.7 12.7 %copy.40 = bf16[1,768,2,1536]{1,3,2,0:T(8,128)(2,1)} copy(bf16[1,768,2,1536]{3,2,0,1:T(2,128)(2,1)} %all-gather.8.cloned.1.call-done) | data formatting | bytes 9437184 | tf_op jit(solution)/shard_map/all_gather | solution.py:51
  112.4 4.7 fusion.225
  117.1 305.1 %all-gather.6.cloned.1.call-done = bf16[1,6144,1536]{2,1,0:T(8,128)(2,1)} async-done(((bf16[1,1536,1536]{2,1,0:T(8,128)(2,1)}), bf16[1,6144,1536]{2,1,0:T(8,128)(2,1)}) %all-gather.6.cloned.1.call-update) | async-done | bytes 18874384 | tf_op jit(solution)/shard_map/all_gather | solution.py:50
  422.2 10.0 %fusion.135 = bf16[8,12,8,128]{3,2,1,0:T(8,128)(2,1)S(1)} fusion(bf16[1,6144,1536]{2,1,0:T(8,128)(2,1)} %all-gather.6.cloned.1.call-done, bf16[1,64,6144]{2,1,0:T(8,128)(2,1)S(1)} %all-gather, f32[6144]{0:T(1024)S(1)} %bitcast.307, f32[64]{0:T(128)S(1)} %add_rsqrt_fusion.5), kind=kOutput, calls=%fused_computation.133 | convolution fusion | flops 1209630720 | bytes 19882240 | tf_op jit(solution)/shard_map/dot_general | solution.py:65
  435.7 2.5 all_gather.45
  438.4 4.2 bitcast_dynamic-update-slice_fusion
  442.7 1.3 collective-permute-start
  445.7 9.5 %collective-permute-done = bf16[64,3072]{1,0:T(8,128)(2,1)} collective-permute-done((bf16[64,3072]{1,0:T(8,128)(2,1)}, bf16[64,3072]{1,0:T(8,128)(2,1)}, u32[]{:S(2)}, u32[]{:S(2)}) %collective-permute-start) | collective-permute-done | bytes 393248 | tf_op jit(solution)/shard_map/ppermute | solution.py:12
  455.2 1.2 bitcast_select_fusion.8
  456.4 3.4 all_gather.46
  460.1 10.0 %fusion.132 = bf16[8,12,8,128]{3,2,1,0:T(8,128)(2,1)S(1)} fusion(bf16[1,6144,1536]{2,1,0:T(8,128)(2,1)} %all-gather.6.cloned.1.call-done, bf16[64,6144]{1,0:T(8,128)(2,1)S(1)} %all_gather.46, f32[64]{0:T(128)S(1)} %add_rsqrt_fusion.4, f32[6144]{0:T(1024)S(1)} %bitcast.308), kind=kOutput, calls=%fused_computation.132 | convolution fusion | flops 1209630720 | bytes 19882240 | tf_op jit(solution)/shard_map/dot_general | solution.py:65
  472.4 1.1 fusion.143
  473.6 2.1 all_gather.47
  475.7 4.3 fusion.182
  480.0 1.3 collective-permute-start.1
  483.0 9.5 %collective-permute-done.1 = bf16[64,3072]{1,0:T(8,128)(2,1)} collective-permute-done((bf16[64,3072]{1,0:T(8,128)(2,1)}, bf16[64,3072]{1,0:T(8,128)(2,1)}, u32[]{:S(2)}, u32[]{:S(2)}) %collective-permute-start.1) | collective-permute-done | bytes 393248 | tf_op jit(solution)/shard_map/ppermute | solution.py:12
  492.5 1.2 bitcast_select_fusion.6
  493.7 3.4 all_gather.48
  497.5 10.0 %fusion.129 = bf16[8,12,8,128]{3,2,1,0:T(8,128)(2,1)S(1)} fusion(bf16[1,6144,1536]{2,1,0:T(8,128)(2,1)} %all-gather.6.cloned.1.call-done, bf16[64,6144]{1,0:T(8,128)(2,1)S(1)} %all_gather.48, f32[64]{0:T(128)S(1)} %add_rsqrt_fusion.3, f32[6144]{0:T(1024)S(1)} %bitcast.309), kind=kOutput, calls=%fused_computation.131 | convolution fusion | flops 1209630720 | bytes 19882240 | tf_op jit(solution)/shard_map/dot_general | solution.py:65
  509.8 1.1 fusion.146
  510.9 2.1 all_gather.49
  513.1 4.3 fusion.181
  517.4 1.3 collective-permute-start.2
  520.6 10.3 %collective-permute-done.2 = bf16[64,3072]{1,0:T(8,128)(2,1)} collective-permute-done((bf16[64,3072]{1,0:T(8,128)(2,1)}, bf16[64,3072]{1,0:T(8,128)(2,1)}, u32[]{:S(2)}, u32[]{:S(2)}) %collective-permute-start.2) | collective-permute-done | bytes 393248 | tf_op jit(solution)/shard_map/ppermute | solution.py:12
  530.8 1.2 bitcast_select_fusion.4
  532.0 3.3 all_gather.50
  535.6 10.0 %fusion.126 = bf16[8,12,8,128]{3,2,1,0:T(8,128)(2,1)S(1)} fusion(bf16[1,6144,1536]{2,1,0:T(8,128)(2,1)} %all-gather.6.cloned.1.call-done, bf16[64,6144]{1,0:T(8,128)(2,1)S(1)} %all_gather.50, f32[64]{0:T(128)S(1)} %add_rsqrt_fusion.2, f32[6144]{0:T(1024)S(1)} %bitcast.310), kind=kOutput, calls=%fused_computation.130 | convolution fusion | flops 1209630720 | bytes 19882240 | tf_op jit(solution)/shard_map/dot_general | solution.py:65
  548.0 1.1 fusion.149
  549.1 2.1 all_gather.51
  551.3 4.3 fusion.180
  555.6 1.3 collective-permute-start.3
  558.8 10.5 %collective-permute-done.3 = bf16[64,3072]{1,0:T(8,128)(2,1)} collective-permute-done((bf16[64,3072]{1,0:T(8,128)(2,1)}, bf16[64,3072]{1,0:T(8,128)(2,1)}, u32[]{:S(2)}, u32[]{:S(2)}) %collective-permute-start.3) | collective-permute-done | bytes 393248 | tf_op jit(solution)/shard_map/ppermute | solution.py:12
  569.3 1.2 bitcast_select_fusion.2
  570.5 3.1 all_gather.52
  573.8 10.0 %fusion.123 = bf16[8,12,8,128]{3,2,1,0:T(8,128)(2,1)S(1)} fusion(bf16[1,6144,1536]{2,1,0:T(8,128)(2,1)} %all-gather.6.cloned.1.call-done, bf16[64,6144]{1,0:T(8,128)(2,1)S(1)} %all_gather.52, f32[64]{0:T(128)S(1)} %add_rsqrt_fusion.1, f32[6144]{0:T(1024)S(1)} %bitcast.311), kind=kOutput, calls=%fused_computation.129 | convolution fusion | flops 1209630720 | bytes 19882240 | tf_op jit(solution)/shard_map/dot_general | solution.py:65
  586.2 1.1 fusion.152
  587.3 2.1 all_gather.53
  589.5 4.3 fusion.179
  593.7 1.3 collective-permute-start.4
  598.0 9.5 %collective-permute-done.4 = bf16[64,3072]{1,0:T(8,128)(2,1)} collective-permute-done((bf16[64,3072]{1,0:T(8,128)(2,1)}, bf16[64,3072]{1,0:T(8,128)(2,1)}, u32[]{:S(2)}, u32[]{:S(2)}) %collective-permute-start.4) | collective-permute-done | bytes 393248 | tf_op jit(solution)/shard_map/ppermute | solution.py:12
  607.5 1.2 bitcast_select_fusion
  608.6 3.1 all_gather.54
  612.1 10.0 %fusion.120 = bf16[8,12,8,128]{3,2,1,0:T(8,128)(2,1)S(1)} fusion(bf16[1,6144,1536]{2,1,0:T(8,128)(2,1)} %all-gather.6.cloned.1.call-done, bf16[64,6144]{1,0:T(8,128)(2,1)S(1)} %all_gather.54, f32[64]{0:T(128)S(1)} %add_rsqrt_fusion, f32[6144]{0:T(1024)S(1)} %bitcast.312), kind=kOutput, calls=%fused_computation.128 | convolution fusion | flops 1209630720 | bytes 19882240 | tf_op jit(solution)/shard_map/dot_general | solution.py:65
  624.4 1.1 fusion.155
  625.5 2.1 all_gather.55
  627.7 4.3 fusion.178
  (146 shorter events, 26.5 us)
Async XLA Ops:
  6.5 93.1 %all-gather.8.cloned.1.call-start = ((), (), s32[]{:S(2)}) async-start(), calls=%async_computation.1 | async-start | bytes 5898240 | tf_op jit(solution)/shard_map/all_gather | solution.py:51
  7.3 9.0 %copy-start.15 = (s32[3]{0:T(128)S(1)}, s32[3]{0:T(128)}, u32[]{:S(2)}) copy-start(s32[3]{0:T(128)} %param.9) | copy-start | bytes 40
  7.3 414.9 %all-gather.6.cloned.1.call-start = ((), (), s32[]{:S(2)}) async-start(), calls=%async_computation | async-start | bytes 23592960 | tf_op jit(solution)/shard_map/all_gather | solution.py:50
  112.4 309.8 %copy-start = (f32[1,6144]{1,0:T(1,128)S(1)}, f32[1,6144]{1,0:T(1,128)}, u32[]{:S(2)}) copy-start(f32[1,6144]{1,0:T(1,128)} %param.11) | copy-start | bytes 73732
  422.2 16.1 %slice-start = ((s8[18874368]{0:T(1024)(128)(4,1)}), s8[4194304]{0:T(1024)(128)(4,1)S(1)}, s32[]{:S(2)}) async-start(s8[18874368]{0:T(1024)(128)(4,1)} %bitcast.287), calls=%async_computation.2 | async-start | bytes 8388608
  422.2 16.2 %slice-start.1 = ((s8[18874368]{0:T(1024)(128)(4,1)}), s8[4194304]{0:T(1024)(128)(4,1)S(1)}, s32[]{:S(2)}) async-start(s8[18874368]{0:T(1024)(128)(4,1)} %bitcast.287), calls=%async_computation.3 | async-start | bytes 8388608
  422.2 16.2 %slice-start.2 = ((s8[18874368]{0:T(1024)(128)(4,1)}), s8[4194304]{0:T(1024)(128)(4,1)S(1)}, s32[]{:S(2)}) async-start(s8[18874368]{0:T(1024)(128)(4,1)} %bitcast.287), calls=%async_computation.4 | async-start | bytes 8388608
  422.2 16.2 %slice-start.3 = ((s8[18874368]{0:T(1024)(128)(4,1)}), s8[4194304]{0:T(1024)(128)(4,1)S(1)}, s32[]{:S(2)}) async-start(s8[18874368]{0:T(1024)(128)(4,1)} %bitcast.287), calls=%async_computation.5 | async-start | bytes 8388608
  432.9 1.7 copy-start.8
  434.6 3.9 slice-start.4
  435.7 2.8 copy-start.7
  442.7 12.5 %collective-permute-start = (bf16[64,3072]{1,0:T(8,128)(2,1)}, bf16[64,3072]{1,0:T(8,128)(2,1)}, u32[]{:S(2)}, u32[]{:S(2)}) collective-permute-start(bf16[64,3072]{1,0:T(8,128)(2,1)} %get-tuple-element.36), channel_id=1, source_target_pairs={{0,8},{8,16},{16,24},{1,9},{9,17},{17,25},{2,10},{10,18},{18,26},{... | collective-permute-start | bytes 1179656 | tf_op jit(solution)/shard_map/ppermute | solution.py:12
  445.1 14.9 %copy-start.1 = (f32[1,6144]{1,0:T(1,128)S(1)}, f32[1,6144]{1,0:T(1,128)}, u32[]{:S(2)}) copy-start(f32[1,6144]{1,0:T(1,128)} %param.11) | copy-start | bytes 73732
  460.0 15.6 %slice-start.5 = ((s8[18874368]{0:T(1024)(128)(4,1)}), s8[4194304]{0:T(1024)(128)(4,1)S(1)}, s32[]{:S(2)}) async-start(s8[18874368]{0:T(1024)(128)(4,1)} %bitcast.289), calls=%async_computation.7 | async-start | bytes 8388608
  460.1 15.6 %slice-start.6 = ((s8[18874368]{0:T(1024)(128)(4,1)}), s8[4194304]{0:T(1024)(128)(4,1)S(1)}, s32[]{:S(2)}) async-start(s8[18874368]{0:T(1024)(128)(4,1)} %bitcast.289), calls=%async_computation.8 | async-start | bytes 8388608
  460.1 15.6 %slice-start.7 = ((s8[18874368]{0:T(1024)(128)(4,1)}), s8[4194304]{0:T(1024)(128)(4,1)S(1)}, s32[]{:S(2)}) async-start(s8[18874368]{0:T(1024)(128)(4,1)} %bitcast.289), calls=%async_computation.9 | async-start | bytes 8388608
  460.1 15.6 %slice-start.8 = ((s8[18874368]{0:T(1024)(128)(4,1)}), s8[4194304]{0:T(1024)(128)(4,1)S(1)}, s32[]{:S(2)}) async-start(s8[18874368]{0:T(1024)(128)(4,1)} %bitcast.289), calls=%async_computation.10 | async-start | bytes 8388608
  470.8 1.7 copy-start.9
  470.8 4.9 slice-start.9
  480.0 12.5 %collective-permute-start.1 = (bf16[64,3072]{1,0:T(8,128)(2,1)}, bf16[64,3072]{1,0:T(8,128)(2,1)}, u32[]{:S(2)}, u32[]{:S(2)}) collective-permute-start(bf16[64,3072]{1,0:T(8,128)(2,1)} %get-tuple-element.12), channel_id=1, source_target_pairs={{0,8},{8,16},{16,24},{1,9},{9,17},{17,25},{2,10},{10,18},{18,26},{... | collective-permute-start | bytes 1179656 | tf_op jit(solution)/shard_map/ppermute | solution.py:12
  482.4 15.0 %copy-start.2 = (f32[1,6144]{1,0:T(1,128)S(1)}, f32[1,6144]{1,0:T(1,128)}, u32[]{:S(2)}) copy-start(f32[1,6144]{1,0:T(1,128)} %param.11) | copy-start | bytes 73732
  497.4 15.6 %slice-start.10 = ((s8[18874368]{0:T(1024)(128)(4,1)}), s8[4194304]{0:T(1024)(128)(4,1)S(1)}, s32[]{:S(2)}) async-start(s8[18874368]{0:T(1024)(128)(4,1)} %bitcast.291), calls=%async_computation.12 | async-start | bytes 8388608
  497.4 15.6 %slice-start.11 = ((s8[18874368]{0:T(1024)(128)(4,1)}), s8[4194304]{0:T(1024)(128)(4,1)S(1)}, s32[]{:S(2)}) async-start(s8[18874368]{0:T(1024)(128)(4,1)} %bitcast.291), calls=%async_computation.13 | async-start | bytes 8388608
  497.4 15.6 %slice-start.12 = ((s8[18874368]{0:T(1024)(128)(4,1)}), s8[4194304]{0:T(1024)(128)(4,1)S(1)}, s32[]{:S(2)}) async-start(s8[18874368]{0:T(1024)(128)(4,1)} %bitcast.291), calls=%async_computation.14 | async-start | bytes 8388608
  497.4 15.6 %slice-start.13 = ((s8[18874368]{0:T(1024)(128)(4,1)}), s8[4194304]{0:T(1024)(128)(4,1)S(1)}, s32[]{:S(2)}) async-start(s8[18874368]{0:T(1024)(128)(4,1)} %bitcast.291), calls=%async_computation.15 | async-start | bytes 8388608
  508.1 1.7 copy-start.10
  508.1 4.9 slice-start.14
  517.4 13.5 %collective-permute-start.2 = (bf16[64,3072]{1,0:T(8,128)(2,1)}, bf16[64,3072]{1,0:T(8,128)(2,1)}, u32[]{:S(2)}, u32[]{:S(2)}) collective-permute-start(bf16[64,3072]{1,0:T(8,128)(2,1)} %get-tuple-element.10), channel_id=1, source_target_pairs={{0,8},{8,16},{16,24},{1,9},{9,17},{17,25},{2,10},{10,18},{18,26},{... | collective-permute-start | bytes 1179656 | tf_op jit(solution)/shard_map/ppermute | solution.py:12
  519.9 15.7 %copy-start.3 = (f32[1,6144]{1,0:T(1,128)S(1)}, f32[1,6144]{1,0:T(1,128)}, u32[]{:S(2)}) copy-start(f32[1,6144]{1,0:T(1,128)} %param.11) | copy-start | bytes 73732
  535.6 15.6 %slice-start.15 = ((s8[18874368]{0:T(1024)(128)(4,1)}), s8[4194304]{0:T(1024)(128)(4,1)S(1)}, s32[]{:S(2)}) async-start(s8[18874368]{0:T(1024)(128)(4,1)} %bitcast.293), calls=%async_computation.17 | async-start | bytes 8388608
  535.6 15.6 %slice-start.16 = ((s8[18874368]{0:T(1024)(128)(4,1)}), s8[4194304]{0:T(1024)(128)(4,1)S(1)}, s32[]{:S(2)}) async-start(s8[18874368]{0:T(1024)(128)(4,1)} %bitcast.293), calls=%async_computation.18 | async-start | bytes 8388608
  535.6 15.6 %slice-start.17 = ((s8[18874368]{0:T(1024)(128)(4,1)}), s8[4194304]{0:T(1024)(128)(4,1)S(1)}, s32[]{:S(2)}) async-start(s8[18874368]{0:T(1024)(128)(4,1)} %bitcast.293), calls=%async_computation.19 | async-start | bytes 8388608
  535.6 15.6 %slice-start.18 = ((s8[18874368]{0:T(1024)(128)(4,1)}), s8[4194304]{0:T(1024)(128)(4,1)S(1)}, s32[]{:S(2)}) async-start(s8[18874368]{0:T(1024)(128)(4,1)} %bitcast.293), calls=%async_computation.20 | async-start | bytes 8388608
  546.3 4.9 slice-start.19
  555.6 13.7 %collective-permute-start.3 = (bf16[64,3072]{1,0:T(8,128)(2,1)}, bf16[64,3072]{1,0:T(8,128)(2,1)}, u32[]{:S(2)}, u32[]{:S(2)}) collective-permute-start(bf16[64,3072]{1,0:T(8,128)(2,1)} %get-tuple-element.8), channel_id=1, source_target_pairs={{0,8},{8,16},{16,24},{1,9},{9,17},{17,25},{2,10},{10,18},{18,26},{... | collective-permute-start | bytes 1179656 | tf_op jit(solution)/shard_map/ppermute | solution.py:12
  558.1 15.7 %copy-start.4 = (f32[1,6144]{1,0:T(1,128)S(1)}, f32[1,6144]{1,0:T(1,128)}, u32[]{:S(2)}) copy-start(f32[1,6144]{1,0:T(1,128)} %param.11) | copy-start | bytes 73732
  573.8 15.6 %slice-start.20 = ((s8[18874368]{0:T(1024)(128)(4,1)}), s8[4194304]{0:T(1024)(128)(4,1)S(1)}, s32[]{:S(2)}) async-start(s8[18874368]{0:T(1024)(128)(4,1)} %bitcast.295), calls=%async_computation.22 | async-start | bytes 8388608
  573.8 15.6 %slice-start.21 = ((s8[18874368]{0:T(1024)(128)(4,1)}), s8[4194304]{0:T(1024)(128)(4,1)S(1)}, s32[]{:S(2)}) async-start(s8[18874368]{0:T(1024)(128)(4,1)} %bitcast.295), calls=%async_computation.23 | async-start | bytes 8388608
  573.8 15.6 %slice-start.22 = ((s8[18874368]{0:T(1024)(128)(4,1)}), s8[4194304]{0:T(1024)(128)(4,1)S(1)}, s32[]{:S(2)}) async-start(s8[18874368]{0:T(1024)(128)(4,1)} %bitcast.295), calls=%async_computation.24 | async-start | bytes 8388608
  573.8 15.6 %slice-start.23 = ((s8[18874368]{0:T(1024)(128)(4,1)}), s8[4194304]{0:T(1024)(128)(4,1)S(1)}, s32[]{:S(2)}) async-start(s8[18874368]{0:T(1024)(128)(4,1)} %bitcast.295), calls=%async_computation.25 | async-start | bytes 8388608
  584.5 4.9 slice-start.24
  593.7 13.7 %collective-permute-start.4 = (bf16[64,3072]{1,0:T(8,128)(2,1)}, bf16[64,3072]{1,0:T(8,128)(2,1)}, u32[]{:S(2)}, u32[]{:S(2)}) collective-permute-start(bf16[64,3072]{1,0:T(8,128)(2,1)} %get-tuple-element.6), channel_id=1, source_target_pairs={{0,8},{8,16},{16,24},{1,9},{9,17},{17,25},{2,10},{10,18},{18,26},{... | collective-permute-start | bytes 1179656 | tf_op jit(solution)/shard_map/ppermute | solution.py:12
  597.0 15.0 %copy-start.5 = (f32[1,6144]{1,0:T(1,128)S(1)}, f32[1,6144]{1,0:T(1,128)}, u32[]{:S(2)}) copy-start(f32[1,6144]{1,0:T(1,128)} %param.11) | copy-start | bytes 73732
  612.0 15.6 %slice-start.25 = ((s8[18874368]{0:T(1024)(128)(4,1)}), s8[4194304]{0:T(1024)(128)(4,1)S(1)}, s32[]{:S(2)}) async-start(s8[18874368]{0:T(1024)(128)(4,1)} %bitcast.297), calls=%async_computation.27 | async-start | bytes 8388608
  612.0 15.6 %slice-start.26 = ((s8[18874368]{0:T(1024)(128)(4,1)}), s8[4194304]{0:T(1024)(128)(4,1)S(1)}, s32[]{:S(2)}) async-start(s8[18874368]{0:T(1024)(128)(4,1)} %bitcast.297), calls=%async_computation.28 | async-start | bytes 8388608
  612.0 15.6 %slice-start.27 = ((s8[18874368]{0:T(1024)(128)(4,1)}), s8[4194304]{0:T(1024)(128)(4,1)S(1)}, s32[]{:S(2)}) async-start(s8[18874368]{0:T(1024)(128)(4,1)} %bitcast.297), calls=%async_computation.29 | async-start | bytes 8388608
  612.0 15.6 %slice-start.28 = ((s8[18874368]{0:T(1024)(128)(4,1)}), s8[4194304]{0:T(1024)(128)(4,1)S(1)}, s32[]{:S(2)}) async-start(s8[18874368]{0:T(1024)(128)(4,1)} %bitcast.297), calls=%async_computation.30 | async-start | bytes 8388608
  622.7 4.9 slice-start.29
  (5 other events, 6.6 us)
Sparse Core Ops, SparseCore 0:
  8.9 90.6 all-gather.7
  101.2 320.9 all-gather.5
where the time goes:
time: 649 us; the launch traced here: 639 us
  waiting for transfers between devices  428 us (66%)
  matrix products  96.2 us (15%)
  between operations  33.1 us (5%)
  blocking collectives  32 us (5%)
  local copies, waits for them, and re-layouts  26.8 us (4%)
  other arithmetic  16.5 us (3%)
    all_gather x1, waiting for transfers between devices, body(): w_whole = lax.all_gather(w_local, 'seq', axis=0, tiled=True)  305 us
    all_gather x1, waiting for transfers between devices, body(): kv_whole = lax.all_gather(kv_local, 'seq', axis=0, tiled=True)  72.3 us
    dot_general x6, matrix products, body(): query = jnp.dot(normed, w_whole, preferred_element_type=jnp.float32)  60 us
    ppermute x5, waiting for transfers between devices, passed_along(): return lax.ppermute(block, axis, route)  49.2 us
    dot_general x6, matrix products, body(): jnp.dot(lax.all_gather(attended, 'mp', axis=1, tiled=True), out_weight, p...  25.6 us
    all_gather x6, blocking collectives, body(): whole = lax.all_gather(current, 'mp', axis=1, tiled=True)  19 us
  transfers between devices with their start and end apart: 7, of which 7 were waited for; matrix products, arithmetic and copies ran while one was open for 4% of the time, Pallas kernels for 0%

commit v1 on v0

--- a/solution.py
+++ b/solution.py
@@ -1,9 +1,14 @@
+import functools
 import jax
 import jax.numpy as jnp
 from jax import lax
+from jax.experimental import pallas as pl
+from jax.experimental.pallas import tpu as pltpu
 from jax.sharding import PartitionSpec as P
 
 HEAD_DIM = 128
+SPLIT = 2
+MESH = pl.DeviceIdType.MESH
 
 
 def passed_along(block, axis, distance):
@@ -38,7 +43,7 @@
     return jnp.transpose(result, (1, 0, 2)).reshape(tokens, heads * width).astype(jnp.bfloat16)
 
 
-def body(video, caption_kv, caption_lengths, order, gains, w_query, w_out):
+def general(video, caption_kv, caption_lengths, order, gains, w_query, w_out):
     samples = video.shape[0]
     segments = lax.axis_size("segment")
     here = lax.axis_index("segment")
@@ -80,6 +85,350 @@
     return section_out[None]
 
 
+def relay_kernel(cfg, bounds, x0, gain_ref, kv_ref, wq_ref, wout_ref, out_ref,
+                 res, xg, qs, qr, ts, tr, ats, atr, flat, kvb, wqv, woutv,
+                 load_sem, kv_send, kv_recv, rel_send, rel_recv, x_send, x_recv, f_send,
+                 q_send, q_recv, t_send, t_recv, a_send, a_recv, b_send, b_recv):
+    segments, seq, chunks, tl, split = cfg
+    blocks = seq // 2
+    g = lax.axis_index("segment")
+    s = lax.axis_index("seq")
+    c = lax.axis_index("mp")
+    width = xg.shape[-1]
+    cols = qs.shape[-1]
+    half = res.shape[-1]
+    tokens = seq * tl
+    hub = s // blocks == c
+    sibling = {"mp": 1 - c}
+
+    def remote(src, dst, send, recv, device):
+        return pltpu.make_async_remote_copy(
+            src_ref=src, dst_ref=dst, send_sem=send, recv_sem=recv,
+            device_id=device, device_id_type=MESH)
+
+    def peers(fn):
+        for off in range(1, seq):
+            fn(lax.rem(s + off, seq))
+
+    def kv_copy(d):
+        return remote(kv_ref.at[d], kvb.at[s], kv_send.at[d], kv_recv.at[s], {"seq": d})
+
+    def kv_arrival(d):
+        return remote(kv_ref.at[d], kvb.at[d], kv_send.at[d], kv_recv.at[d], {"seq": d})
+
+    def rel_copy(k, j):
+        part = pl.ds(j * width, width)
+        return remote(out_ref.at[k, :, part], res.at[k, :, part],
+                      rel_send.at[k, j], rel_recv.at[k, j], {"segment": g + 1})
+
+    def x_copy(k, j):
+        part = pl.ds(j * width, width)
+        return remote(res.at[k, :, part], xg.at[k, s], x_send.at[k, j], x_recv.at[k, s],
+                      {"seq": blocks * c + j})
+
+    def forward_copy(k, d):
+        return remote(xg.at[k, d], xg.at[k, d], f_send.at[k, d], x_recv.at[k, d], sibling)
+
+    def q_copy(k, d):
+        return remote(qs.at[k, d], qr.at[k, s], q_send.at[k, d], q_recv.at[k, s], {"seq": d})
+
+    def q_arrival(k, d):
+        return remote(qs.at[k, d], qr.at[k, d], q_send.at[k, d], q_recv.at[k, d], {"seq": d})
+
+    def t_copy(k, d):
+        return remote(ts.at[k], tr.at[k, s], t_send.at[k, d], t_recv.at[k, s], {"seq": d})
+
+    def t_arrival(k, d):
+        return remote(ts.at[k], tr.at[k, d], t_send.at[k, d], t_recv.at[k, d], {"seq": d})
+
+    def a_copy(k, d):
+        return remote(ats.at[k, d], atr.at[k, c, s], a_send.at[k, d], a_recv.at[k, s], {"seq": d})
+
+    def a_arrival(k, d):
+        return remote(ats.at[k, d], atr.at[k, c, d], a_send.at[k, d], a_recv.at[k, d], {"seq": d})
+
+    def b_copy(k, d):
+        return remote(atr.at[k, c, d], atr.at[k, c, d], b_send.at[k, d], b_recv.at[k, d], sibling)
+
+    def b_arrival(k, d):
+        return remote(atr.at[k, 1 - c, d], atr.at[k, 1 - c, d], b_send.at[k, d], b_recv.at[k, d], sibling)
+
+    load_wq = pltpu.make_async_copy(wq_ref, wqv, load_sem.at[0])
+    load_wout = pltpu.make_async_copy(wout_ref, woutv, load_sem.at[1])
+    load_kv = pltpu.make_async_copy(kv_ref.at[s], kvb.at[s], load_sem.at[2])
+    load_x = pltpu.make_async_copy(x0, res, load_sem.at[3])
+
+    @pl.when(g == 0)
+    def _():
+        load_x.start()
+
+    load_wq.start()
+    load_kv.start()
+    load_wout.start()
+
+    barrier = pltpu.get_barrier_semaphore()
+
+    def greet(device):
+        pl.semaphore_signal(barrier, inc=1, device_id=device, device_id_type=MESH)
+
+    peers(lambda d: greet({"seq": d}))
+    greet(sibling)
+
+    @pl.when(g > 0)
+    def _():
+        greet({"segment": g - 1})
+
+    @pl.when(g < segments - 1)
+    def _():
+        greet({"segment": g + 1})
+
+    inner = (g > 0) & (g < segments - 1)
+
+    @pl.when(inner)
+    def _():
+        pl.semaphore_wait(barrier, seq + 2)
+
+    @pl.when(jnp.logical_not(inner))
+    def _():
+        pl.semaphore_wait(barrier, seq + 1)
+
+    @pl.when(g == 0)
+    def _():
+        load_x.wait()
+
+    def send_x(k):
+        for j in range(blocks):
+            @pl.when(g > 0)
+            def _():
+                remote(out_ref.at[k, :, pl.ds(j * width, width)], res.at[k, :, pl.ds(j * width, width)],
+                       rel_send.at[k, j], rel_recv.at[k, j], {"segment": g - 1}).wait_recv()
+
+            mine = blocks * c + j == s
+
+            @pl.when(mine)
+            def _():
+                xg[k, s] = res[k, :, j * width:(j + 1) * width]
+                forward_copy(k, s).start()
+
+            @pl.when(jnp.logical_not(mine))
+            def _():
+                x_copy(k, j).start()
+
+    def collect_x(k):
+        @pl.when(hub)
+        def _():
+            def one(d):
+                forward_copy(k, d).wait_recv()
+                forward_copy(k, d).start()
+            peers(one)
+
+        @pl.when(jnp.logical_not(hub))
+        def _():
+            for d in range(seq):
+                forward_copy(k, d).wait_recv()
+
+    def project(k):
+        x = xg[k].reshape(tokens, width).astype(jnp.float32)
+        square = jnp.sum(x * x, axis=-1, keepdims=True)
+        ts[k] = jnp.transpose(jnp.broadcast_to(square, (tokens, 128)))[:8]
+        y = (x * gain_ref[:, pl.ds(pl.multiple_of(s * width, width), width)]).astype(jnp.bfloat16)
+
+        def one(d):
+            t_copy(k, d).start()
+            w = wqv[:, pl.ds(pl.multiple_of(d * cols, cols), cols)]
+            qs[k, d] = jnp.dot(y, w, preferred_element_type=jnp.float32).astype(jnp.bfloat16)
+            q_copy(k, d).start()
+        peers(one)
+        w = wqv[:, pl.ds(pl.multiple_of(s * cols, cols), cols)]
+        qr[k, s] = jnp.dot(y, w, preferred_element_type=jnp.float32).astype(jnp.bfloat16)
+        tr[k, s] = ts[k]
+
+    def attend(k):
+        def arrived(d):
+            t_arrival(k, d).wait_recv()
+            q_arrival(k, d).wait_recv()
+        peers(arrived)
+        square = jnp.sum(tr[k], axis=0)[:1]
+        square = jnp.transpose(jnp.broadcast_to(square, (128, tokens)))
+        scale = lax.rsqrt(square / (seq * width) + 1e-6)
+        total = qr[k, 0].astype(jnp.float32)
+        for d in range(1, seq):
+            total = total + qr[k, d].astype(jnp.float32)
+        micro = k // split
+        first, last = bounds[0, micro], bounds[1, micro]
+        rows = kvb.shape[2] * seq
+        index = lax.broadcasted_iota(jnp.int32, (1, rows), 1)
+        valid = (index >= first) & (index < last)
+        for h in range(cols // HEAD_DIM):
+            part = slice(h * HEAD_DIM, (h + 1) * HEAD_DIM)
+            q = (total[:, part] * scale).astype(jnp.bfloat16)
+            keys = kvb[:, 0, :, part].reshape(rows, HEAD_DIM)
+            values = kvb[:, 1, :, part].reshape(rows, HEAD_DIM)
+            scores = lax.dot_general(q, keys, (((1,), (1,)), ((), ())),
+                                     preferred_element_type=jnp.float32) * HEAD_DIM ** (-0.5)
+            scores = jnp.where(valid, scores, -1e30)
+            top = jnp.max(scores, axis=-1, keepdims=True)
+            weights = jnp.exp(scores - top)
+            norm = jnp.sum(weights, axis=-1, keepdims=True)
+            acc = jnp.dot(weights.astype(jnp.bfloat16), values, preferred_element_type=jnp.float32)
+            ats[k, :, :, part] = (acc / norm).astype(jnp.bfloat16).reshape(seq, tl, HEAD_DIM)
+        peers(lambda d: a_copy(k, d).start())
+        atr[k, c, s] = ats[k, s]
+        b_copy(k, s).start()
+
+    def finish_chunk(k):
+        def one(d):
+            a_arrival(k, d).wait_recv()
+            b_copy(k, d).start()
+        peers(one)
+        for d in range(seq):
+            b_arrival(k, d).wait_recv()
+        for e in range(2):
+            for d in range(seq):
+                at = (e * seq + d) * cols
+                flat[:, at:at + cols] = atr[k, e, d]
+        tile = 512
+        for j in range(blocks):
+            def step(n, carry):
+                place = pl.ds(pl.multiple_of(j * width + n * tile, tile), tile)
+                acc = jnp.dot(flat[...], woutv[:, place], preferred_element_type=jnp.float32)
+                out_ref[k, :, place] = (res[k, :, place].astype(jnp.float32) + acc).astype(jnp.bfloat16)
+                return carry
+            lax.fori_loop(0, width // tile, step, 0)
+
+            @pl.when(g < segments - 1)
+            def _():
+                rel_copy(k, j).start()
+
+    def tick(i, carry):
+        @pl.when(i < chunks)
+        def _():
+            send_x(i)
+
+        @pl.when(i == 0)
+        def _():
+            peers(lambda d: kv_copy(d).start())
+
+        @pl.when(i == 1)
+        def _():
+            load_wout.wait()
+
+        @pl.when(i > 0)
+        def _():
+            finish_chunk(i - 1)
+
+        @pl.when(i == 0)
+        def _():
+            load_wq.wait()
+
+        @pl.when(i < chunks)
+        def _():
+            collect_x(i)
+            project(i)
+
+        @pl.when(i == 0)
+        def _():
+            load_kv.wait()
+            peers(lambda d: kv_arrival(d).wait_recv())
+
+        @pl.when(i < chunks)
+        def _():
+            attend(i)
+        return carry
+
+    lax.fori_loop(0, chunks + 1, tick, 0)
+
+    def drain(k, carry):
+        for j in range(blocks):
+            @pl.when(blocks * c + j != s)
+            def _():
+                x_copy(k, j).wait_send()
+
+            @pl.when(g < segments - 1)
+            def _():
+                rel_copy(k, j).wait_send()
+
+        @pl.when(hub)
+        def _():
+            for d in range(seq):
+                forward_copy(k, d).wait_send()
+
+        def one(d):
+            q_copy(k, d).wait_send()
+            t_copy(k, d).wait_send()
+            a_copy(k, d).wait_send()
+        peers(one)
+        for d in range(seq):
+            b_copy(k, d).wait_send()
+        return carry
+
+    lax.fori_loop(0, chunks, drain, 0)
+    peers(lambda d: kv_copy(d).wait_send())
+
+
+def relay(video, caption_kv, caption_lengths, order, gains, w_query, w_out):
+    samples, local, half = video.shape
+    segments = lax.axis_size("segment")
+    seq = lax.axis_size("seq")
+    split = SPLIT
+    chunks, tl = samples * split, local // split
+    tokens = seq * tl
+    rows = caption_kv.shape[1]
+    width, cols_all = w_query.shape[1:]
+    cols = cols_all // seq
+    blocks = seq // 2
+    ends = jnp.cumsum(caption_lengths)
+    bounds = jnp.stack([ends - caption_lengths, ends])[:, order].astype(jnp.int32)
+    x0 = jnp.take(video, order, axis=0).reshape(chunks, tl, half)
+    kv = caption_kv[0].reshape(rows, 2, seq, cols).transpose(2, 1, 0, 3)
+    bf = jnp.bfloat16
+    dma = pltpu.SemaphoreType.DMA
+    hbm = pl.BlockSpec(memory_space=pl.ANY)
+    out = pl.pallas_call(
+        functools.partial(relay_kernel, (segments, seq, chunks, tl, split)),
+        out_shape=jax.ShapeDtypeStruct((chunks, tl, half), bf),
+        in_specs=[pl.BlockSpec(memory_space=pltpu.SMEM), hbm,
+                  pl.BlockSpec(memory_space=pltpu.VMEM), hbm, hbm, hbm],
+        out_specs=pl.BlockSpec(memory_space=pltpu.VMEM),
+        scratch_shapes=[
+            pltpu.VMEM((chunks, tl, half), bf),
+            pltpu.VMEM((chunks, seq, tl, width), bf),
+            pltpu.VMEM((chunks, seq, tokens, cols), bf),
+            pltpu.VMEM((chunks, seq, tokens, cols), bf),
+            pltpu.VMEM((chunks, 8, tokens), jnp.float32),
+            pltpu.VMEM((chunks, seq, 8, tokens), jnp.float32),
+            pltpu.VMEM((chunks, seq, tl, cols), bf),
+            pltpu.VMEM((chunks, 2, seq, tl, cols), bf),
+            pltpu.VMEM((tl, 2 * seq * cols), bf),
+            pltpu.VMEM((seq, 2, rows, cols), bf),
+            pltpu.VMEM((width, cols_all), bf),
+            pltpu.VMEM(w_out.shape[1:], bf),
+            dma((4,)), dma((seq,)), dma((seq,)),
+            dma((chunks, blocks)), dma((chunks, blocks)),
+            dma((chunks, blocks)), dma((chunks, seq)), dma((chunks, seq)),
+            dma((chunks, seq)), dma((chunks, seq)), dma((chunks, seq)), dma((chunks, seq)),
+            dma((chunks, seq)), dma((chunks, seq)), dma((chunks, seq)), dma((chunks, seq)),
+        ],
+        compiler_params=pltpu.CompilerParams(
+            collective_id=0, has_side_effects=True, vmem_limit_bytes=58 * 2 ** 20),
+    )(bounds, x0, gains, kv, w_query[0], w_out[0])
+    return out.reshape(1, samples, local, half)
+
+
+def body(video, caption_kv, caption_lengths, order, gains, w_query, w_out):
+    seq = lax.axis_size("seq")
+    fits = (
+        lax.axis_size("mp") == 2 and seq % 2 == 0
+        and w_query.shape[2] % (seq * HEAD_DIM) == 0
+        and w_query.shape[1] % 512 == 0
+        and (video.shape[1] // SPLIT) % 16 == 0 and caption_kv.shape[1] % 16 == 0
+        and (seq * video.shape[1] // SPLIT) % 128 == 0
+        and w_out.shape[1] * w_out.shape[2] <= 3072 * 3072
+    )
+    run = relay if fits else general
+    return run(video, caption_kv, caption_lengths, order, gains, w_query, w_out)
+
+
 def solution(mesh):
     in_specs = (
         P(None, "seq", "mp"),

time: 649 us -> 337 us (0.52); the launches traced: 639 us -> 337 us
  waiting for transfers between devices: 428 us -> 0 us
  Pallas kernels: 0 us -> 325 us
  matrix products: 96.2 us -> 0 us
  between operations: 33.1 us -> 0.04 us
  blocking collectives: 32 us -> 0 us
  local copies, waits for them, and re-layouts: 26.8 us -> 6.88 us
  other arithmetic: 16.5 us -> 4.17 us
    all_gather x2 -> x0, waiting for transfers between devices: 377 us -> none  [the longest x1 305 us: body(): w_whole = lax.all_gather(w_local, 'seq', axis=0, tiled=True)]
    pallas_call x0 -> x1, Pallas kernels: none -> 325 us  [relay(): pl.pallas_call(functools.partial(relay_kernel, (segments, seq, chunks, tl...]
    dot_general x24 -> x0, matrix products: 96.2 us -> none  [the longest x6 60 us: body(): query = jnp.dot(normed, w_whole, preferred_element_type=jnp.float32)]
    ppermute x5 -> x0, waiting for transfers between devices: 49.2 us -> none  [passed_along(): return lax.ppermute(block, axis, route)]
    all_gather x12 -> x0, blocking collectives: 32 us -> none  [the longest x6 19 us: body(): whole = lax.all_gather(current, 'mp', axis=1, tiled=True)]
    all_gather x1 -> x0, local copies, waits for them, and re-layouts: 12.7 us -> none  [body(): kv_whole = lax.all_gather(kv_local, 'seq', axis=0, tiled=True)]
  transfers between devices with their start and end apart: 7 -> 0, of which waited for: 7 -> 0; matrix products, arithmetic and copies ran while one was open for 4% -> 0% of each run, Pallas kernels for 0% -> 0%
where the time goes in v1:
time: 337 us
  Pallas kernels  325 us (96%)
  local copies, waits for them, and re-layouts  6.88 us (2%)
  other arithmetic  4.17 us (1%)
    pallas_call x1, Pallas kernels, relay(): pl.pallas_call(functools.partial(relay_kernel, (segments, seq, chunks, tl...  325 us

profile of v1, /device:TPU:7, one launch (start us, length us, event | category | flops | bytes accessed | tf_op | source)
XLA Modules:
  0.0 336.6 jit_solution(17594894074338237810)
XLA Ops:
  0.0 0.0 copy-start
  0.0 0.9 reduce-window.4
  0.9 0.7 fusion
  1.6 0.7 compare_and_fusion
  2.2 0.1 broadcast_in_dim.18
  2.3 0.1 broadcast_in_dim.19
  2.4 0.7 compare_select_fusion
  3.1 0.1 copy.11
  3.2 0.1 copy.12
  3.3 0.1 pad_add_fusion
  3.3 0.6 gather_fusion
  3.9 0.6 copy.13
  4.5 0.0 copy-done
  4.5 0.6 gather_fusion.1
  5.1 0.0 copy-start.1
  5.1 1.2 broadcast_select_fusion.x0
  6.3 0.5 copy-done.1
  6.8 0.8 reshape.39
  7.6 1.2 copy.19
  8.7 325.5 %shard_map.73 = bf16[6,32,3072]{2,1,0:T(8,128)(2,1)} custom-call(s32[2,3]{1,0:T(2,128)} %bitcast.21, bf16[6,32,3072]{2,1,0:T(8,128)(2,1)} %broadcast_select_fusion.x0, f32[1,6144]{1,0:T(1,128)} %gain_ref.1, bf16[4,2,192,384]{3,2,1,0:T(8,128)(2,1)} %bitcast.17, bf16[1536,1536]{1,0:T(8,128)(2,1)} %bitcast.20, bf16[3072,3072]{1,0:T(8,128)(2,1)} %bitcast.16), custom_call_target="tpu_custom_call" | custom-call | tf_op jit(solution)/shard_map/pallas_call | solution.py:387
  334.2 2.4 copy.21
  (1 shorter events, 0.0 us)
Async XLA Ops:
  0.0 4.5 %copy-start = (bf16[3,64,3072]{2,1,0:T(8,128)(2,1)S(1)}, bf16[3,64,3072]{2,1,0:T(8,128)(2,1)}, u32[]{:S(2)}) copy-start(bf16[3,64,3072]{2,1,0:T(8,128)(2,1)} %param.7) | copy-start | bytes 3538948
  5.1 1.7 copy-start.1

commit v2 on v1

--- a/solution.py
+++ b/solution.py
@@ -85,9 +85,9 @@
     return section_out[None]
 
 
-def relay_kernel(cfg, bounds, x0, gain_ref, kv_ref, wq_ref, wout_ref, out_ref,
+def relay_kernel(cfg, lengths, order, video_ref, gain_ref, kv_ref, wq_ref, wout_ref, out_ref,
                  res, xg, qs, qr, ts, tr, ats, atr, flat, kvb, wqv, woutv,
-                 load_sem, kv_send, kv_recv, rel_send, rel_recv, x_send, x_recv, f_send,
+                 load_sem, kv_send, kv_recv, rel_send, res_send, res_recv, x_send, x_recv, f_send,
                  q_send, q_recv, t_send, t_recv, a_send, a_recv, b_send, b_recv):
     segments, seq, chunks, tl, split = cfg
     blocks = seq // 2
@@ -116,10 +116,15 @@
     def kv_arrival(d):
         return remote(kv_ref.at[d], kvb.at[d], kv_send.at[d], kv_recv.at[d], {"seq": d})
 
-    def rel_copy(k, j):
-        part = pl.ds(j * width, width)
-        return remote(out_ref.at[k, :, part], res.at[k, :, part],
-                      rel_send.at[k, j], rel_recv.at[k, j], {"segment": g + 1})
+    def next_copy(k, j):
+        return remote(out_ref.at[k, :, pl.ds(j * width, width)], xg.at[k, s],
+                      rel_send.at[k, j], x_recv.at[k, s], {"segment": g + 1, "seq": blocks * c + j})
+
+    def res_copy(k):
+        return remote(out_ref.at[k], res.at[k], res_send.at[k], res_recv.at[k], {"segment": g + 1})
+
+    def res_arrival(k):
+        return remote(out_ref.at[k], res.at[k], res_send.at[k], res_recv.at[k], {"segment": g - 1})
 
     def x_copy(k, j):
         part = pl.ds(j * width, width)
@@ -156,11 +161,6 @@
     load_wq = pltpu.make_async_copy(wq_ref, wqv, load_sem.at[0])
     load_wout = pltpu.make_async_copy(wout_ref, woutv, load_sem.at[1])
     load_kv = pltpu.make_async_copy(kv_ref.at[s], kvb.at[s], load_sem.at[2])
-    load_x = pltpu.make_async_copy(x0, res, load_sem.at[3])
-
-    @pl.when(g == 0)
-    def _():
-        load_x.start()
 
     load_wq.start()
     load_kv.start()
@@ -174,35 +174,43 @@
     peers(lambda d: greet({"seq": d}))
     greet(sibling)
 
-    @pl.when(g > 0)
+    @pl.when((g > 0) & hub)
+    def _():
+        for d in range(seq):
+            greet({"segment": g - 1, "seq": d})
+
+    @pl.when((g > 0) & jnp.logical_not(hub))
     def _():
         greet({"segment": g - 1})
 
-    @pl.when(g < segments - 1)
-    def _():
-        greet({"segment": g + 1})
-
-    inner = (g > 0) & (g < segments - 1)
-
-    @pl.when(inner)
-    def _():
-        pl.semaphore_wait(barrier, seq + 2)
-
-    @pl.when(jnp.logical_not(inner))
-    def _():
-        pl.semaphore_wait(barrier, seq + 1)
+    ahead = g < segments - 1
+
+    @pl.when(jnp.logical_not(ahead))
+    def _():
+        pl.semaphore_wait(barrier, seq)
+
+    @pl.when(ahead & hub)
+    def _():
+        pl.semaphore_wait(barrier, seq + blocks)
+
+    @pl.when(ahead & jnp.logical_not(hub))
+    def _():
+        pl.semaphore_wait(barrier, seq + blocks + 1)
 
     @pl.when(g == 0)
     def _():
-        load_x.wait()
+        def choose(k, carry):
+            rows = pl.ds(pl.multiple_of(lax.rem(k, split) * tl, tl), tl)
+            sample = order[k // split]
+            picked = video_ref[0, rows, :]
+            for b in range(1, video_ref.shape[0]):
+                picked = jnp.where(sample == b, video_ref[b, rows, :], picked)
+            res[k] = picked
+            return carry
+        lax.fori_loop(0, chunks, choose, 0)
 
     def send_x(k):
         for j in range(blocks):
-            @pl.when(g > 0)
-            def _():
-                remote(out_ref.at[k, :, pl.ds(j * width, width)], res.at[k, :, pl.ds(j * width, width)],
-                       rel_send.at[k, j], rel_recv.at[k, j], {"segment": g - 1}).wait_recv()
-
             mine = blocks * c + j == s
 
             @pl.when(mine)
@@ -221,6 +229,10 @@
                 forward_copy(k, d).wait_recv()
                 forward_copy(k, d).start()
             peers(one)
+
+            @pl.when(g > 0)
+            def _():
+                one(s)
 
         @pl.when(jnp.logical_not(hub))
         def _():
@@ -255,7 +267,11 @@
         for d in range(1, seq):
             total = total + qr[k, d].astype(jnp.float32)
         micro = k // split
-        first, last = bounds[0, micro], bounds[1, micro]
+        sample = order[micro]
+        first = jnp.int32(0)
+        for b in range(video_ref.shape[0] - 1):
+            first = first + jnp.where(b < sample, lengths[b], 0)
+        last = first + lengths[sample]
         rows = kvb.shape[2] * seq
         index = lax.broadcasted_iota(jnp.int32, (1, rows), 1)
         valid = (index >= first) & (index < last)
@@ -288,6 +304,11 @@
                 at = (e * seq + d) * cols
                 flat[:, at:at + cols] = atr[k, e, d]
         tile = 512
+
+        @pl.when(g > 0)
+        def _():
+            res_arrival(k).wait_recv()
+
         for j in range(blocks):
             def step(n, carry):
                 place = pl.ds(pl.multiple_of(j * width + n * tile, tile), tile)
@@ -298,24 +319,20 @@
 
             @pl.when(g < segments - 1)
             def _():
-                rel_copy(k, j).start()
+                next_copy(k, j).start()
+
+        @pl.when(g < segments - 1)
+        def _():
+            res_copy(k).start()
 
     def tick(i, carry):
-        @pl.when(i < chunks)
+        @pl.when((i < chunks) & (g == 0))
         def _():
             send_x(i)
 
         @pl.when(i == 0)
         def _():
             peers(lambda d: kv_copy(d).start())
-
-        @pl.when(i == 1)
-        def _():
-            load_wout.wait()
-
-        @pl.when(i > 0)
-        def _():
-            finish_chunk(i - 1)
 
         @pl.when(i == 0)
         def _():
@@ -326,6 +343,14 @@
             collect_x(i)
             project(i)
 
+        @pl.when(i == 1)
+        def _():
+            load_wout.wait()
+
+        @pl.when(i > 0)
+        def _():
+            finish_chunk(i - 1)
+
         @pl.when(i == 0)
         def _():
             load_kv.wait()
@@ -340,13 +365,17 @@
 
     def drain(k, carry):
         for j in range(blocks):
-            @pl.when(blocks * c + j != s)
+            @pl.when((g == 0) & (blocks * c + j != s))
             def _():
                 x_copy(k, j).wait_send()
 
             @pl.when(g < segments - 1)
             def _():
-                rel_copy(k, j).wait_send()
+                next_copy(k, j).wait_send()
+
+        @pl.when(g < segments - 1)
+        def _():
+            res_copy(k).wait_send()
 
         @pl.when(hub)
         def _():
@@ -377,19 +406,17 @@
     width, cols_all = w_query.shape[1:]
     cols = cols_all // seq
     blocks = seq // 2
-    ends = jnp.cumsum(caption_lengths)
-    bounds = jnp.stack([ends - caption_lengths, ends])[:, order].astype(jnp.int32)
-    x0 = jnp.take(video, order, axis=0).reshape(chunks, tl, half)
     kv = caption_kv[0].reshape(rows, 2, seq, cols).transpose(2, 1, 0, 3)
     bf = jnp.bfloat16
     dma = pltpu.SemaphoreType.DMA
     hbm = pl.BlockSpec(memory_space=pl.ANY)
+    vmem = pl.BlockSpec(memory_space=pltpu.VMEM)
+    scalars = pl.BlockSpec(memory_space=pltpu.SMEM)
     out = pl.pallas_call(
         functools.partial(relay_kernel, (segments, seq, chunks, tl, split)),
         out_shape=jax.ShapeDtypeStruct((chunks, tl, half), bf),
-        in_specs=[pl.BlockSpec(memory_space=pltpu.SMEM), hbm,
-                  pl.BlockSpec(memory_space=pltpu.VMEM), hbm, hbm, hbm],
-        out_specs=pl.BlockSpec(memory_space=pltpu.VMEM),
+        in_specs=[scalars, scalars, vmem, vmem, hbm, hbm, hbm],
+        out_specs=vmem,
         scratch_shapes=[
             pltpu.VMEM((chunks, tl, half), bf),
             pltpu.VMEM((chunks, seq, tl, width), bf),
@@ -403,15 +430,15 @@
             pltpu.VMEM((seq, 2, rows, cols), bf),
             pltpu.VMEM((width, cols_all), bf),
             pltpu.VMEM(w_out.shape[1:], bf),
-            dma((4,)), dma((seq,)), dma((seq,)),
-            dma((chunks, blocks)), dma((chunks, blocks)),
+            dma((3,)), dma((seq,)), dma((seq,)),
+            dma((chunks, blocks)), dma((chunks,)), dma((chunks,)),
             dma((chunks, blocks)), dma((chunks, seq)), dma((chunks, seq)),
             dma((chunks, seq)), dma((chunks, seq)), dma((chunks, seq)), dma((chunks, seq)),
             dma((chunks, seq)), dma((chunks, seq)), dma((chunks, seq)), dma((chunks, seq)),
         ],
         compiler_params=pltpu.CompilerParams(
             collective_id=0, has_side_effects=True, vmem_limit_bytes=58 * 2 ** 20),
-    )(bounds, x0, gains, kv, w_query[0], w_out[0])
+    )(caption_lengths, order, video, gains, kv, w_query[0], w_out[0])
     return out.reshape(1, samples, local, half)
 
 

time: 337 us -> 275 us (0.82)
  Pallas kernels: 325 us -> 268 us
  other arithmetic: 4.17 us -> 0 us
    pallas_call x1, Pallas kernels: 325 us -> 268 us  [relay(): pl.pallas_call(functools.partial(relay_kernel, (segments, seq, chunks, tl...]
where the time goes in v2:
time: 275 us
  Pallas kernels  268 us (97%)
  local copies, waits for them, and re-layouts  6.95 us (3%)
    pallas_call x1, Pallas kernels, relay(): pl.pallas_call(functools.partial(relay_kernel, (segments, seq, chunks, tl...  268 us

profile of v2, /device:TPU:7, one launch (start us, length us, event | category | flops | bytes accessed | tf_op | source)
XLA Modules:
  0.0 274.6 jit_solution(14455367338311991307)
XLA Ops:
  0.0 3.4 %reshape.4 = bf16[192,2,4,384]{3,2,1,0:T(4,128)(2,1)S(1)} reshape(bf16[1,192,2,1536]{3,2,1,0:T(2,128)(2,1)} %param.8) | data formatting | bytes 2359296 | tf_op jit(solution)/shard_map/reshape;squeeze | solution.py:409
  3.4 1.2 copy.13
  4.6 267.7 %shard_map.73 = bf16[6,32,3072]{2,1,0:T(8,128)(2,1)} custom-call(s32[3]{0:T(128)} %lengths.1, s32[3]{0:T(128)} %order.1, bf16[3,64,3072]{2,1,0:T(8,128)(2,1)} %video_ref.1, f32[1,6144]{1,0:T(1,128)} %gain_ref.1, bf16[4,2,192,384]{3,2,1,0:T(8,128)(2,1)} %bitcast.7, bf16[1536,1536]{1,0:T(8,128)(2,1)} %bitcast.9, bf16[3072,3072]{1,0:T(8,128)(2,1)} %bitcast.6), custom_call_target="tpu_custom_call" | custom-call | tf_op jit(solution)/shard_map/pallas_call | solution.py:415
  272.3 2.4 copy.15

commit v3 on v2

--- a/solution.py
+++ b/solution.py
@@ -326,9 +326,9 @@
             res_copy(k).start()
 
     def tick(i, carry):
-        @pl.when((i < chunks) & (g == 0))
-        def _():
-            send_x(i)
+        @pl.when((i == 0) & (g == 0))
+        def _():
+            send_x(0)
 
         @pl.when(i == 0)
         def _():
@@ -342,6 +342,10 @@
         def _():
             collect_x(i)
             project(i)
+
+        @pl.when((i < chunks - 1) & (g == 0))
+        def _():
+            send_x(i + 1)
 
         @pl.when(i == 1)
         def _():

time: 275 us -> 255 us (0.927)
  Pallas kernels: 268 us -> 248 us
    pallas_call x1, Pallas kernels: 268 us -> 248 us  [relay(): pl.pallas_call(functools.partial(relay_kernel, (segments, seq, chunks, tl...]
where the time goes in v3:
time: 255 us
  Pallas kernels  248 us (97%)
  local copies, waits for them, and re-layouts  6.95 us (3%)
    pallas_call x1, Pallas kernels, relay(): pl.pallas_call(functools.partial(relay_kernel, (segments, seq, chunks, tl...  248 us

profile of v3, /device:TPU:7, one launch (start us, length us, event | category | flops | bytes accessed | tf_op | source)
XLA Modules:
  0.0 255.1 jit_solution(14337522918264670347)
XLA Ops:
  0.0 3.4 %reshape.4 = bf16[192,2,4,384]{3,2,1,0:T(4,128)(2,1)S(1)} reshape(bf16[1,192,2,1536]{3,2,1,0:T(2,128)(2,1)} %param.8) | data formatting | bytes 2359296 | tf_op jit(solution)/shard_map/reshape;squeeze | solution.py:413
  3.4 1.2 copy.13
  4.6 248.1 %shard_map.73 = bf16[6,32,3072]{2,1,0:T(8,128)(2,1)} custom-call(s32[3]{0:T(128)} %lengths.1, s32[3]{0:T(128)} %order.1, bf16[3,64,3072]{2,1,0:T(8,128)(2,1)} %video_ref.1, f32[1,6144]{1,0:T(1,128)} %gain_ref.1, bf16[4,2,192,384]{3,2,1,0:T(8,128)(2,1)} %bitcast.7, bf16[1536,1536]{1,0:T(8,128)(2,1)} %bitcast.9, bf16[3072,3072]{1,0:T(8,128)(2,1)} %bitcast.6), custom_call_target="tpu_custom_call" | custom-call | tf_op jit(solution)/shard_map/pallas_call | solution.py:419
  252.7 2.4 copy.15

commit v4 on v3

--- a/solution.py
+++ b/solution.py
@@ -110,14 +110,23 @@
         for off in range(1, seq):
             fn(lax.rem(s + off, seq))
 
+    def kv_part(d):
+        return kv_ref.at[:, :, pl.ds(pl.multiple_of(d * cols, cols), cols)]
+
     def kv_copy(d):
-        return remote(kv_ref.at[d], kvb.at[s], kv_send.at[d], kv_recv.at[s], {"seq": d})
+        return remote(kv_part(d), kvb.at[s], kv_send.at[d], kv_recv.at[s], {"seq": d})
 
     def kv_arrival(d):
-        return remote(kv_ref.at[d], kvb.at[d], kv_send.at[d], kv_recv.at[d], {"seq": d})
+        return remote(kv_part(d), kvb.at[d], kv_send.at[d], kv_recv.at[d], {"seq": d})
 
     def next_copy(k, j):
         return remote(out_ref.at[k, :, pl.ds(j * width, width)], xg.at[k, s],
+                      rel_send.at[k, j], x_recv.at[k, s], {"segment": g + 1, "seq": blocks * c + j})
+
+    def next_tile(k, j, n, tile):
+        place = pl.ds(pl.multiple_of(n * tile, tile), tile)
+        source = pl.ds(pl.multiple_of(j * width + n * tile, tile), tile)
+        return remote(out_ref.at[k, :, source], xg.at[k, s, :, place],
                       rel_send.at[k, j], x_recv.at[k, s], {"segment": g + 1, "seq": blocks * c + j})
 
     def res_copy(k):
@@ -160,7 +169,7 @@
 
     load_wq = pltpu.make_async_copy(wq_ref, wqv, load_sem.at[0])
     load_wout = pltpu.make_async_copy(wout_ref, woutv, load_sem.at[1])
-    load_kv = pltpu.make_async_copy(kv_ref.at[s], kvb.at[s], load_sem.at[2])
+    load_kv = pltpu.make_async_copy(kv_part(s), kvb.at[s], load_sem.at[2])
 
     load_wq.start()
     load_kv.start()
@@ -222,17 +231,22 @@
             def _():
                 x_copy(k, j).start()
 
+    def pass_on(k, own):
+        def one(d):
+            forward_copy(k, d).wait_recv()
+            forward_copy(k, d).start()
+        peers(one)
+        if own:
+            one(s)
+
     def collect_x(k):
-        @pl.when(hub)
-        def _():
-            def one(d):
-                forward_copy(k, d).wait_recv()
-                forward_copy(k, d).start()
-            peers(one)
-
-            @pl.when(g > 0)
-            def _():
-                one(s)
+        @pl.when(hub & (g > 0))
+        def _():
+            pass_on(k, True)
+
+        @pl.when(hub & (g == 0) & (k == 0))
+        def _():
+            pass_on(k, False)
 
         @pl.when(jnp.logical_not(hub))
         def _():
@@ -314,13 +328,13 @@
                 place = pl.ds(pl.multiple_of(j * width + n * tile, tile), tile)
                 acc = jnp.dot(flat[...], woutv[:, place], preferred_element_type=jnp.float32)
                 out_ref[k, :, place] = (res[k, :, place].astype(jnp.float32) + acc).astype(jnp.bfloat16)
+
+                @pl.when(g < segments - 1)
+                def _():
+                    next_tile(k, j, n, tile).start()
                 return carry
             lax.fori_loop(0, width // tile, step, 0)
 
-            @pl.when(g < segments - 1)
-            def _():
-                next_copy(k, j).start()
-
         @pl.when(g < segments - 1)
         def _():
             res_copy(k).start()
@@ -334,6 +348,10 @@
         def _():
             peers(lambda d: kv_copy(d).start())
 
+        @pl.when((i == 0) & (g == 0))
+        def _():
+            send_x(1)
+
         @pl.when(i == 0)
         def _():
             load_wq.wait()
@@ -343,9 +361,9 @@
             collect_x(i)
             project(i)
 
-        @pl.when((i < chunks - 1) & (g == 0))
-        def _():
-            send_x(i + 1)
+        @pl.when((i < chunks - 2) & (g == 0))
+        def _():
+            send_x(i + 2)
 
         @pl.when(i == 1)
         def _():
@@ -363,6 +381,10 @@
         @pl.when(i < chunks)
         def _():
             attend(i)
+
+        @pl.when((i < chunks - 1) & (g == 0) & hub)
+        def _():
+            pass_on(i + 1, False)
         return carry
 
     lax.fori_loop(0, chunks + 1, tick, 0)
@@ -410,7 +432,7 @@
     width, cols_all = w_query.shape[1:]
     cols = cols_all // seq
     blocks = seq // 2
-    kv = caption_kv[0].reshape(rows, 2, seq, cols).transpose(2, 1, 0, 3)
+    kv = caption_kv[0].transpose(1, 0, 2)
     bf = jnp.bfloat16
     dma = pltpu.SemaphoreType.DMA
     hbm = pl.BlockSpec(memory_space=pl.ANY)

time: 255 us -> 274 us (1.075)
  Pallas kernels: 248 us -> 269 us
    pallas_call x1, Pallas kernels: 248 us -> 269 us  [relay(): pl.pallas_call(functools.partial(relay_kernel, (segments, seq, chunks, tl...]
    another operation x2 -> x0, local copies, waits for them, and re-layouts: 4.59 us -> none  [relay(): kv = caption_kv[0].reshape(rows, 2, seq, cols).transpose(2, 1, 0, 3)]
where the time goes in v4:
time: 274 us
  Pallas kernels  269 us (98%)
  local copies, waits for them, and re-layouts  4.76 us (2%)
    pallas_call x1, Pallas kernels, relay(): pl.pallas_call(functools.partial(relay_kernel, (segments, seq, chunks, tl...  269 us

profile of v4, /device:TPU:7, one launch (start us, length us, event | category | flops | bytes accessed | tf_op | source)
XLA Modules:
  0.0 274.3 jit_solution(10980712679416162869)
XLA Ops:
  0.0 2.4 copy.10
  2.4 269.5 %shard_map.73 = bf16[6,32,3072]{2,1,0:T(8,128)(2,1)} custom-call(s32[3]{0:T(128)} %lengths.1, s32[3]{0:T(128)} %order.1, bf16[3,64,3072]{2,1,0:T(8,128)(2,1)} %video_ref.1, f32[1,6144]{1,0:T(1,128)} %gain_ref.1, bf16[2,192,1536]{2,1,0:T(8,128)(2,1)} %bitcast.10, bf16[1536,1536]{1,0:T(8,128)(2,1)} %bitcast.11, bf16[3072,3072]{1,0:T(8,128)(2,1)} %bitcast.8), custom_call_target="tpu_custom_call" | custom-call | tf_op jit(solution)/shard_map/pallas_call | solution.py:441
  271.9 2.4 copy.12

commit v5 on v4

--- a/solution.py
+++ b/solution.py
@@ -86,9 +86,9 @@
 
 
 def relay_kernel(cfg, lengths, order, video_ref, gain_ref, kv_ref, wq_ref, wout_ref, out_ref,
-                 res, xg, qs, qr, ts, tr, ats, atr, flat, kvb, wqv, woutv,
-                 load_sem, kv_send, kv_recv, rel_send, res_send, res_recv, x_send, x_recv, f_send,
-                 q_send, q_recv, t_send, t_recv, a_send, a_recv, b_send, b_recv):
+                 res, xg, qs, qr, ats, atr, flat, kvb, wqv, woutv,
+                 load_sem, kv_send, kv_recv, rel_send, res_send, res_recv, x_send, x_recv, f_send, f_recv,
+                 q_send, q_recv, a_send, a_recv, b_send, b_recv):
     segments, seq, chunks, tl, split = cfg
     blocks = seq // 2
     g = lax.axis_index("segment")
@@ -123,12 +123,6 @@
         return remote(out_ref.at[k, :, pl.ds(j * width, width)], xg.at[k, s],
                       rel_send.at[k, j], x_recv.at[k, s], {"segment": g + 1, "seq": blocks * c + j})
 
-    def next_tile(k, j, n, tile):
-        place = pl.ds(pl.multiple_of(n * tile, tile), tile)
-        source = pl.ds(pl.multiple_of(j * width + n * tile, tile), tile)
-        return remote(out_ref.at[k, :, source], xg.at[k, s, :, place],
-                      rel_send.at[k, j], x_recv.at[k, s], {"segment": g + 1, "seq": blocks * c + j})
-
     def res_copy(k):
         return remote(out_ref.at[k], res.at[k], res_send.at[k], res_recv.at[k], {"segment": g + 1})
 
@@ -140,8 +134,11 @@
         return remote(res.at[k, :, part], xg.at[k, s], x_send.at[k, j], x_recv.at[k, s],
                       {"seq": blocks * c + j})
 
-    def forward_copy(k, d):
-        return remote(xg.at[k, d], xg.at[k, d], f_send.at[k, d], x_recv.at[k, d], sibling)
+    def x_arrival(k, d):
+        return remote(xg.at[k, d], xg.at[k, d], x_send.at[k, 0], x_recv.at[k, d], {"seq": d})
+
+    def forward_copy(k):
+        return remote(xg.at[k], xg.at[k], f_send.at[k], f_recv.at[k], sibling)
 
     def q_copy(k, d):
         return remote(qs.at[k, d], qr.at[k, s], q_send.at[k, d], q_recv.at[k, s], {"seq": d})
@@ -149,23 +146,17 @@
     def q_arrival(k, d):
         return remote(qs.at[k, d], qr.at[k, d], q_send.at[k, d], q_recv.at[k, d], {"seq": d})
 
-    def t_copy(k, d):
-        return remote(ts.at[k], tr.at[k, s], t_send.at[k, d], t_recv.at[k, s], {"seq": d})
-
-    def t_arrival(k, d):
-        return remote(ts.at[k], tr.at[k, d], t_send.at[k, d], t_recv.at[k, d], {"seq": d})
-
     def a_copy(k, d):
         return remote(ats.at[k, d], atr.at[k, c, s], a_send.at[k, d], a_recv.at[k, s], {"seq": d})
 
     def a_arrival(k, d):
         return remote(ats.at[k, d], atr.at[k, c, d], a_send.at[k, d], a_recv.at[k, d], {"seq": d})
 
-    def b_copy(k, d):
-        return remote(atr.at[k, c, d], atr.at[k, c, d], b_send.at[k, d], b_recv.at[k, d], sibling)
-
-    def b_arrival(k, d):
-        return remote(atr.at[k, 1 - c, d], atr.at[k, 1 - c, d], b_send.at[k, d], b_recv.at[k, d], sibling)
+    def b_copy(k):
+        return remote(atr.at[k, c], atr.at[k, c], b_send.at[k], b_recv.at[k], sibling)
+
+    def b_arrival(k):
+        return remote(atr.at[k, 1 - c], atr.at[k, 1 - c], b_send.at[k], b_recv.at[k], sibling)
 
     load_wq = pltpu.make_async_copy(wq_ref, wqv, load_sem.at[0])
     load_wout = pltpu.make_async_copy(wout_ref, woutv, load_sem.at[1])
@@ -225,19 +216,16 @@
             @pl.when(mine)
             def _():
                 xg[k, s] = res[k, :, j * width:(j + 1) * width]
-                forward_copy(k, s).start()
 
             @pl.when(jnp.logical_not(mine))
             def _():
                 x_copy(k, j).start()
 
     def pass_on(k, own):
-        def one(d):
-            forward_copy(k, d).wait_recv()
-            forward_copy(k, d).start()
-        peers(one)
+        peers(lambda d: x_arrival(k, d).wait_recv())
         if own:
-            one(s)
+            x_arrival(k, s).wait_recv()
+        forward_copy(k).start()
 
     def collect_x(k):
         @pl.when(hub & (g > 0))
@@ -250,36 +238,38 @@
 
         @pl.when(jnp.logical_not(hub))
         def _():
-            for d in range(seq):
-                forward_copy(k, d).wait_recv()
+            forward_copy(k).wait_recv()
 
     def project(k):
         x = xg[k].reshape(tokens, width).astype(jnp.float32)
         square = jnp.sum(x * x, axis=-1, keepdims=True)
-        ts[k] = jnp.transpose(jnp.broadcast_to(square, (tokens, 128)))[:8]
+        square = jnp.transpose(jnp.broadcast_to(square, (tokens, 128)))[:8]
+        high = square.astype(jnp.bfloat16)
+        low = (square - high.astype(jnp.float32)).astype(jnp.bfloat16)
+        sums = jnp.concatenate([jnp.concatenate([high, low], axis=0)] * (cols // tokens), axis=1)
         y = (x * gain_ref[:, pl.ds(pl.multiple_of(s * width, width), width)]).astype(jnp.bfloat16)
 
         def one(d):
-            t_copy(k, d).start()
             w = wqv[:, pl.ds(pl.multiple_of(d * cols, cols), cols)]
-            qs[k, d] = jnp.dot(y, w, preferred_element_type=jnp.float32).astype(jnp.bfloat16)
+            qs[k, d, :tokens] = jnp.dot(y, w, preferred_element_type=jnp.float32).astype(jnp.bfloat16)
+            qs[k, d, tokens:] = sums
             q_copy(k, d).start()
         peers(one)
         w = wqv[:, pl.ds(pl.multiple_of(s * cols, cols), cols)]
-        qr[k, s] = jnp.dot(y, w, preferred_element_type=jnp.float32).astype(jnp.bfloat16)
-        tr[k, s] = ts[k]
+        qr[k, s, :tokens] = jnp.dot(y, w, preferred_element_type=jnp.float32).astype(jnp.bfloat16)
+        qr[k, s, tokens:] = sums
 
     def attend(k):
         def arrived(d):
-            t_arrival(k, d).wait_recv()
             q_arrival(k, d).wait_recv()
         peers(arrived)
-        square = jnp.sum(tr[k], axis=0)[:1]
+        sums = jnp.sum(qr[k, :, tokens:, :tokens].astype(jnp.float32), axis=0)
+        square = sums[:1] + sums[8:9]
         square = jnp.transpose(jnp.broadcast_to(square, (128, tokens)))
         scale = lax.rsqrt(square / (seq * width) + 1e-6)
-        total = qr[k, 0].astype(jnp.float32)
+        total = qr[k, 0, :tokens].astype(jnp.float32)
         for d in range(1, seq):
-            total = total + qr[k, d].astype(jnp.float32)
+            total = total + qr[k, d, :tokens].astype(jnp.float32)
         micro = k // split
         sample = order[micro]
         first = jnp.int32(0)
@@ -304,15 +294,11 @@
             ats[k, :, :, part] = (acc / norm).astype(jnp.bfloat16).reshape(seq, tl, HEAD_DIM)
         peers(lambda d: a_copy(k, d).start())
         atr[k, c, s] = ats[k, s]
-        b_copy(k, s).start()
 
     def finish_chunk(k):
-        def one(d):
-            a_arrival(k, d).wait_recv()
-            b_copy(k, d).start()
-        peers(one)
-        for d in range(seq):
-            b_arrival(k, d).wait_recv()
+        peers(lambda d: a_arrival(k, d).wait_recv())
+        b_copy(k).start()
+        b_arrival(k).wait_recv()
         for e in range(2):
             for d in range(seq):
                 at = (e * seq + d) * cols
@@ -328,12 +314,12 @@
                 place = pl.ds(pl.multiple_of(j * width + n * tile, tile), tile)
                 acc = jnp.dot(flat[...], woutv[:, place], preferred_element_type=jnp.float32)
                 out_ref[k, :, place] = (res[k, :, place].astype(jnp.float32) + acc).astype(jnp.bfloat16)
-
-                @pl.when(g < segments - 1)
-                def _():
-                    next_tile(k, j, n, tile).start()
                 return carry
             lax.fori_loop(0, width // tile, step, 0)
+
+            @pl.when(g < segments - 1)
+            def _():
+                next_copy(k, j).start()
 
         @pl.when(g < segments - 1)
         def _():
@@ -405,16 +391,13 @@
 
         @pl.when(hub)
         def _():
-            for d in range(seq):
-                forward_copy(k, d).wait_send()
+            forward_copy(k).wait_send()
 
         def one(d):
             q_copy(k, d).wait_send()
-            t_copy(k, d).wait_send()
             a_copy(k, d).wait_send()
         peers(one)
-        for d in range(seq):
-            b_copy(k, d).wait_send()
+        b_copy(k).wait_send()
         return carry
 
     lax.fori_loop(0, chunks, drain, 0)
@@ -446,10 +429,8 @@
         scratch_shapes=[
             pltpu.VMEM((chunks, tl, half), bf),
             pltpu.VMEM((chunks, seq, tl, width), bf),
-            pltpu.VMEM((chunks, seq, tokens, cols), bf),
-            pltpu.VMEM((chunks, seq, tokens, cols), bf),
-            pltpu.VMEM((chunks, 8, tokens), jnp.float32),
-            pltpu.VMEM((chunks, seq, 8, tokens), jnp.float32),
+            pltpu.VMEM((chunks, seq, tokens + 16, cols), bf),
+            pltpu.VMEM((chunks, seq, tokens + 16, cols), bf),
             pltpu.VMEM((chunks, seq, tl, cols), bf),
             pltpu.VMEM((chunks, 2, seq, tl, cols), bf),
             pltpu.VMEM((tl, 2 * seq * cols), bf),
@@ -458,9 +439,9 @@
             pltpu.VMEM(w_out.shape[1:], bf),
             dma((3,)), dma((seq,)), dma((seq,)),
             dma((chunks, blocks)), dma((chunks,)), dma((chunks,)),
-            dma((chunks, blocks)), dma((chunks, seq)), dma((chunks, seq)),
-            dma((chunks, seq)), dma((chunks, seq)), dma((chunks, seq)), dma((chunks, seq)),
-            dma((chunks, seq)), dma((chunks, seq)), dma((chunks, seq)), dma((chunks, seq)),
+            dma((chunks, blocks)), dma((chunks, seq)), dma((chunks,)), dma((chunks,)),
+            dma((chunks, seq)), dma((chunks, seq)),
+            dma((chunks, seq)), dma((chunks, seq)), dma((chunks,)), dma((chunks,)),
         ],
         compiler_params=pltpu.CompilerParams(
             collective_id=0, has_side_effects=True, vmem_limit_bytes=58 * 2 ** 20),
@@ -476,6 +457,7 @@
         and w_query.shape[1] % 512 == 0
         and (video.shape[1] // SPLIT) % 16 == 0 and caption_kv.shape[1] % 16 == 0
         and (seq * video.shape[1] // SPLIT) % 128 == 0
+        and (w_query.shape[2] // seq) % (seq * video.shape[1] // SPLIT) == 0
         and w_out.shape[1] * w_out.shape[2] <= 3072 * 3072
     )
     run = relay if fits else general

time: 274 us -> 272 us (level)
    pallas_call x1, Pallas kernels: 269 us -> 267 us  [relay(): pl.pallas_call(functools.partial(relay_kernel, (segments, seq, chunks, tl...]
where the time goes in v5:
time: 272 us; the launch traced here: 271 us
  Pallas kernels  267 us (98%)
  local copies, waits for them, and re-layouts  4.76 us (2%)
    pallas_call x1, Pallas kernels, relay(): pl.pallas_call(functools.partial(relay_kernel, (segments, seq, chunks, tl...  267 us

profile of v5, /device:TPU:7, one launch (start us, length us, event | category | flops | bytes accessed | tf_op | source)
XLA Modules:
  0.0 271.5 jit_solution(2640395347897160631)
XLA Ops:
  0.0 2.4 copy.10
  2.4 266.7 %shard_map.73 = bf16[6,32,3072]{2,1,0:T(8,128)(2,1)} custom-call(s32[3]{0:T(128)} %lengths.1, s32[3]{0:T(128)} %order.1, bf16[3,64,3072]{2,1,0:T(8,128)(2,1)} %video_ref.1, f32[1,6144]{1,0:T(1,128)} %gain_ref.1, bf16[2,192,1536]{2,1,0:T(8,128)(2,1)} %bitcast.10, bf16[1536,1536]{1,0:T(8,128)(2,1)} %bitcast.11, bf16[3072,3072]{1,0:T(8,128)(2,1)} %bitcast.8), custom_call_target="tpu_custom_call" | custom-call | tf_op jit(solution)/shard_map/pallas_call | solution.py:424
  269.1 2.4 copy.12

commit v6 on v5

--- a/solution.py
+++ b/solution.py
@@ -86,8 +86,8 @@
 
 
 def relay_kernel(cfg, lengths, order, video_ref, gain_ref, kv_ref, wq_ref, wout_ref, out_ref,
-                 res, xg, qs, qr, ats, atr, flat, kvb, wqv, woutv,
-                 load_sem, kv_send, kv_recv, rel_send, res_send, res_recv, x_send, x_recv, f_send, f_recv,
+                 res, xg, qs, qr, ats, atr, flat, kvs, kvb, wqv, woutv,
+                 load_sem, stage_sem, kv_send, kv_recv, rel_send, res_send, res_recv, x_send, x_recv, f_send, f_recv,
                  q_send, q_recv, a_send, a_recv, b_send, b_recv):
     segments, seq, chunks, tl, split = cfg
     blocks = seq // 2
@@ -114,10 +114,10 @@
         return kv_ref.at[:, :, pl.ds(pl.multiple_of(d * cols, cols), cols)]
 
     def kv_copy(d):
-        return remote(kv_part(d), kvb.at[s], kv_send.at[d], kv_recv.at[s], {"seq": d})
+        return remote(kvs.at[d], kvb.at[s], kv_send.at[d], kv_recv.at[s], {"seq": d})
 
     def kv_arrival(d):
-        return remote(kv_part(d), kvb.at[d], kv_send.at[d], kv_recv.at[d], {"seq": d})
+        return remote(kvs.at[d], kvb.at[d], kv_send.at[d], kv_recv.at[d], {"seq": d})
 
     def next_copy(k, j):
         return remote(out_ref.at[k, :, pl.ds(j * width, width)], xg.at[k, s],
@@ -160,10 +160,14 @@
 
     load_wq = pltpu.make_async_copy(wq_ref, wqv, load_sem.at[0])
     load_wout = pltpu.make_async_copy(wout_ref, woutv, load_sem.at[1])
+    def stage(d):
+        return pltpu.make_async_copy(kv_part(d), kvs.at[d], stage_sem.at[d])
+
     load_kv = pltpu.make_async_copy(kv_part(s), kvb.at[s], load_sem.at[2])
 
+    peers(lambda d: stage(d).start())
+    load_kv.start()
     load_wq.start()
-    load_kv.start()
     load_wout.start()
 
     barrier = pltpu.get_barrier_semaphore()
@@ -332,11 +336,10 @@
 
         @pl.when(i == 0)
         def _():
-            peers(lambda d: kv_copy(d).start())
-
-        @pl.when((i == 0) & (g == 0))
-        def _():
-            send_x(1)
+            def one(d):
+                stage(d).wait()
+                kv_copy(d).start()
+            peers(one)
 
         @pl.when(i == 0)
         def _():
@@ -347,9 +350,9 @@
             collect_x(i)
             project(i)
 
-        @pl.when((i < chunks - 2) & (g == 0))
-        def _():
-            send_x(i + 2)
+        @pl.when((i < chunks - 1) & (g == 0))
+        def _():
+            send_x(i + 1)
 
         @pl.when(i == 1)
         def _():
@@ -435,9 +438,10 @@
             pltpu.VMEM((chunks, 2, seq, tl, cols), bf),
             pltpu.VMEM((tl, 2 * seq * cols), bf),
             pltpu.VMEM((seq, 2, rows, cols), bf),
+            pltpu.VMEM((seq, 2, rows, cols), bf),
             pltpu.VMEM((width, cols_all), bf),
             pltpu.VMEM(w_out.shape[1:], bf),
-            dma((3,)), dma((seq,)), dma((seq,)),
+            dma((3,)), dma((seq,)), dma((seq,)), dma((seq,)),
             dma((chunks, blocks)), dma((chunks,)), dma((chunks,)),
             dma((chunks, blocks)), dma((chunks, seq)), dma((chunks,)), dma((chunks,)),
             dma((chunks, seq)), dma((chunks, seq)),

time: 272 us -> 267 us (0.982)
  Pallas kernels: 267 us -> 262 us
    pallas_call x1, Pallas kernels: 267 us -> 262 us  [relay(): pl.pallas_call(functools.partial(relay_kernel, (segments, seq, chunks, tl...]
where the time goes in v6:
time: 267 us
  Pallas kernels  262 us (98%)
  local copies, waits for them, and re-layouts  4.76 us (2%)
    pallas_call x1, Pallas kernels, relay(): pl.pallas_call(functools.partial(relay_kernel, (segments, seq, chunks, tl...  262 us

profile of v6, /device:TPU:7, one launch (start us, length us, event | category | flops | bytes accessed | tf_op | source)
XLA Modules:
  0.0 266.9 jit_solution(4377652139994669909)
XLA Ops:
  0.0 2.4 copy.10
  2.4 262.1 %shard_map.73 = bf16[6,32,3072]{2,1,0:T(8,128)(2,1)} custom-call(s32[3]{0:T(128)} %lengths.1, s32[3]{0:T(128)} %order.1, bf16[3,64,3072]{2,1,0:T(8,128)(2,1)} %video_ref.1, f32[1,6144]{1,0:T(1,128)} %gain_ref.1, bf16[2,192,1536]{2,1,0:T(8,128)(2,1)} %bitcast.10, bf16[1536,1536]{1,0:T(8,128)(2,1)} %bitcast.11, bf16[3072,3072]{1,0:T(8,128)(2,1)} %bitcast.8), custom_call_target="tpu_custom_call" | custom-call | tf_op jit(solution)/shard_map/pallas_call | solution.py:427
  264.5 2.4 copy.12

commit v7 on v4

--- a/solution.py
+++ b/solution.py
@@ -86,8 +86,8 @@
 
 
 def relay_kernel(cfg, lengths, order, video_ref, gain_ref, kv_ref, wq_ref, wout_ref, out_ref,
-                 res, xg, qs, qr, ts, tr, ats, atr, flat, kvb, wqv, woutv,
-                 load_sem, kv_send, kv_recv, rel_send, res_send, res_recv, x_send, x_recv, f_send,
+                 res, xg, qs, qr, ts, tr, ats, atr, flat, kvs, kvb, wqv, woutv,
+                 load_sem, stage_sem, kv_send, kv_recv, rel_send, res_send, res_recv, x_send, x_recv, f_send,
                  q_send, q_recv, t_send, t_recv, a_send, a_recv, b_send, b_recv):
     segments, seq, chunks, tl, split = cfg
     blocks = seq // 2
@@ -114,19 +114,13 @@
         return kv_ref.at[:, :, pl.ds(pl.multiple_of(d * cols, cols), cols)]
 
     def kv_copy(d):
-        return remote(kv_part(d), kvb.at[s], kv_send.at[d], kv_recv.at[s], {"seq": d})
+        return remote(kvs.at[d], kvb.at[s], kv_send.at[d], kv_recv.at[s], {"seq": d})
 
     def kv_arrival(d):
-        return remote(kv_part(d), kvb.at[d], kv_send.at[d], kv_recv.at[d], {"seq": d})
+        return remote(kvs.at[d], kvb.at[d], kv_send.at[d], kv_recv.at[d], {"seq": d})
 
     def next_copy(k, j):
         return remote(out_ref.at[k, :, pl.ds(j * width, width)], xg.at[k, s],
-                      rel_send.at[k, j], x_recv.at[k, s], {"segment": g + 1, "seq": blocks * c + j})
-
-    def next_tile(k, j, n, tile):
-        place = pl.ds(pl.multiple_of(n * tile, tile), tile)
-        source = pl.ds(pl.multiple_of(j * width + n * tile, tile), tile)
-        return remote(out_ref.at[k, :, source], xg.at[k, s, :, place],
                       rel_send.at[k, j], x_recv.at[k, s], {"segment": g + 1, "seq": blocks * c + j})
 
     def res_copy(k):
@@ -169,10 +163,14 @@
 
     load_wq = pltpu.make_async_copy(wq_ref, wqv, load_sem.at[0])
     load_wout = pltpu.make_async_copy(wout_ref, woutv, load_sem.at[1])
+    def stage(d):
+        return pltpu.make_async_copy(kv_part(d), kvs.at[d], stage_sem.at[d])
+
     load_kv = pltpu.make_async_copy(kv_part(s), kvb.at[s], load_sem.at[2])
 
+    peers(lambda d: stage(d).start())
+    load_kv.start()
     load_wq.start()
-    load_kv.start()
     load_wout.start()
 
     barrier = pltpu.get_barrier_semaphore()
@@ -328,13 +326,13 @@
                 place = pl.ds(pl.multiple_of(j * width + n * tile, tile), tile)
                 acc = jnp.dot(flat[...], woutv[:, place], preferred_element_type=jnp.float32)
                 out_ref[k, :, place] = (res[k, :, place].astype(jnp.float32) + acc).astype(jnp.bfloat16)
-
-                @pl.when(g < segments - 1)
-                def _():
-                    next_tile(k, j, n, tile).start()
                 return carry
             lax.fori_loop(0, width // tile, step, 0)
 
+            @pl.when(g < segments - 1)
+            def _():
+                next_copy(k, j).start()
+
         @pl.when(g < segments - 1)
         def _():
             res_copy(k).start()
@@ -346,11 +344,10 @@
 
         @pl.when(i == 0)
         def _():
-            peers(lambda d: kv_copy(d).start())
-
-        @pl.when((i == 0) & (g == 0))
-        def _():
-            send_x(1)
+            def one(d):
+                stage(d).wait()
+                kv_copy(d).start()
+            peers(one)
 
         @pl.when(i == 0)
         def _():
@@ -361,9 +358,9 @@
             collect_x(i)
             project(i)
 
-        @pl.when((i < chunks - 2) & (g == 0))
-        def _():
-            send_x(i + 2)
+        @pl.when((i < chunks - 1) & (g == 0))
+        def _():
+            send_x(i + 1)
 
         @pl.when(i == 1)
         def _():
@@ -454,9 +451,10 @@
             pltpu.VMEM((chunks, 2, seq, tl, cols), bf),
             pltpu.VMEM((tl, 2 * seq * cols), bf),
             pltpu.VMEM((seq, 2, rows, cols), bf),
+            pltpu.VMEM((seq, 2, rows, cols), bf),
             pltpu.VMEM((width, cols_all), bf),
             pltpu.VMEM(w_out.shape[1:], bf),
-            dma((3,)), dma((seq,)), dma((seq,)),
+            dma((3,)), dma((seq,)), dma((seq,)), dma((seq,)),
             dma((chunks, blocks)), dma((chunks,)), dma((chunks,)),
             dma((chunks, blocks)), dma((chunks, seq)), dma((chunks, seq)),
             dma((chunks, seq)), dma((chunks, seq)), dma((chunks, seq)), dma((chunks, seq)),

time: 274 us -> 279 us (1.018)
  Pallas kernels: 269 us -> 274 us
    pallas_call x1, Pallas kernels: 269 us -> 274 us  [relay(): pl.pallas_call(functools.partial(relay_kernel, (segments, seq, chunks, tl...]
where the time goes in v7:
time: 279 us
  Pallas kernels  274 us (98%)
  local copies, waits for them, and re-layouts  4.76 us (2%)
    pallas_call x1, Pallas kernels, relay(): pl.pallas_call(functools.partial(relay_kernel, (segments, seq, chunks, tl...  274 us

profile of v7, /device:TPU:7, one launch (start us, length us, event | category | flops | bytes accessed | tf_op | source)
XLA Modules:
  0.0 278.8 jit_solution(1279129637037037729)
XLA Ops:
  0.0 2.4 copy.10
  2.4 274.1 %shard_map.73 = bf16[6,32,3072]{2,1,0:T(8,128)(2,1)} custom-call(s32[3]{0:T(128)} %lengths.1, s32[3]{0:T(128)} %order.1, bf16[3,64,3072]{2,1,0:T(8,128)(2,1)} %video_ref.1, f32[1,6144]{1,0:T(1,128)} %gain_ref.1, bf16[2,192,1536]{2,1,0:T(8,128)(2,1)} %bitcast.10, bf16[1536,1536]{1,0:T(8,128)(2,1)} %bitcast.11, bf16[3072,3072]{1,0:T(8,128)(2,1)} %bitcast.8), custom_call_target="tpu_custom_call" | custom-call | tf_op jit(solution)/shard_map/pallas_call | solution.py:438
  276.5 2.4 copy.12

commit v8 on v3

--- a/solution.py
+++ b/solution.py
@@ -245,14 +245,28 @@
         ts[k] = jnp.transpose(jnp.broadcast_to(square, (tokens, 128)))[:8]
         y = (x * gain_ref[:, pl.ds(pl.multiple_of(s * width, width), width)]).astype(jnp.bfloat16)
 
-        def one(d):
-            t_copy(k, d).start()
-            w = wqv[:, pl.ds(pl.multiple_of(d * cols, cols), cols)]
-            qs[k, d] = jnp.dot(y, w, preferred_element_type=jnp.float32).astype(jnp.bfloat16)
-            q_copy(k, d).start()
-        peers(one)
-        w = wqv[:, pl.ds(pl.multiple_of(s * cols, cols), cols)]
-        qr[k, s] = jnp.dot(y, w, preferred_element_type=jnp.float32).astype(jnp.bfloat16)
+        peers(lambda d: t_copy(k, d).start())
+        pairs = seq // 2
+        for turn in range(1, pairs + 1):
+            pair = lax.rem(s // 2 + turn, pairs)
+            w = wqv[:, pl.ds(pl.multiple_of(pair * 2 * cols, 2 * cols), 2 * cols)]
+            both = jnp.dot(y, w, preferred_element_type=jnp.float32).astype(jnp.bfloat16)
+            for e in range(2):
+                d = 2 * pair + e
+                block = both[:, e * cols:(e + 1) * cols]
+                if turn < pairs:
+                    qs[k, d] = block
+                    q_copy(k, d).start()
+                    continue
+
+                @pl.when(d == s)
+                def _():
+                    qr[k, s] = block
+
+                @pl.when(d != s)
+                def _():
+                    qs[k, d] = block
+                    q_copy(k, d).start()
         tr[k, s] = ts[k]
 
     def attend(k):
@@ -303,7 +317,7 @@
             for d in range(seq):
                 at = (e * seq + d) * cols
                 flat[:, at:at + cols] = atr[k, e, d]
-        tile = 512
+        tile = 768 if width % 768 == 0 else 512
 
         @pl.when(g > 0)
         def _():

time: 255 us -> 281 us (1.10)
  Pallas kernels: 248 us -> 274 us
    pallas_call x1, Pallas kernels: 248 us -> 274 us  [relay(): pl.pallas_call(functools.partial(relay_kernel, (segments, seq, chunks, tl...]
where the time goes in v8:
time: 281 us
  Pallas kernels  274 us (98%)
  local copies, waits for them, and re-layouts  6.95 us (2%)
    pallas_call x1, Pallas kernels, relay(): pl.pallas_call(functools.partial(relay_kernel, (segments, seq, chunks, tl...  274 us

profile of v8, /device:TPU:7, one launch (start us, length us, event | category | flops | bytes accessed | tf_op | source)
XLA Modules:
  0.0 280.5 jit_solution(10367333995769354277)
XLA Ops:
  0.0 3.4 %reshape.4 = bf16[192,2,4,384]{3,2,1,0:T(4,128)(2,1)S(1)} reshape(bf16[1,192,2,1536]{3,2,1,0:T(2,128)(2,1)} %param.8) | data formatting | bytes 2359296 | tf_op jit(solution)/shard_map/reshape;squeeze | solution.py:427
  3.4 1.2 copy.13
  4.6 273.5 %shard_map.73 = bf16[6,32,3072]{2,1,0:T(8,128)(2,1)} custom-call(s32[3]{0:T(128)} %lengths.1, s32[3]{0:T(128)} %order.1, bf16[3,64,3072]{2,1,0:T(8,128)(2,1)} %video_ref.1, f32[1,6144]{1,0:T(1,128)} %gain_ref.1, bf16[4,2,192,384]{3,2,1,0:T(8,128)(2,1)} %bitcast.7, bf16[1536,1536]{1,0:T(8,128)(2,1)} %bitcast.9, bf16[3072,3072]{1,0:T(8,128)(2,1)} %bitcast.6), custom_call_target="tpu_custom_call" | custom-call | tf_op jit(solution)/shard_map/pallas_call | solution.py:433
  278.1 2.4 copy.15
